TPU v7x, 512 devices: a whole 4x4x16 slice. The times are simulated.
512 devices in a mesh: dom: 128 (over x, z, core), batch: 4 (over y).
Axes of the slice: x: 4, y: 4, z: 16, core: 2. Of those that a mesh axis runs over, the one named last changes fastest.
Arguments:
- features: bfloat16 [128, 1024, 256], P('dom', 'batch'), may hold values from -6 to 6
- initial: bfloat16 [128, 1024, 256], P('dom', 'batch'), may hold values from -6 to 6
- grad_output: bfloat16 [128, 1024, 256], P('dom', 'batch'), may hold values from -6 to 6
- weight: bfloat16 [256, 256], replicated, may hold values from -0.375 to 0.375
- history: bfloat16 [128, 4096, 256], P('dom'), may hold values from -6 to 6
- halo_table: int32 [128, 4, 128, 8], P('dom', 'batch'), may hold values from -1 to 4095, as said below
- tile_cols: int32 [128, 4, 2, 8], P('dom', 'batch'), may hold values from 0 to 9, as said below
- tile_vals: bfloat16 [128, 4, 2, 8, 128, 128], P('dom', 'batch'), may hold values from -0.1875 to 0.1875
- batch_ids: int32 [128, 4, 256], P('dom'), may hold values from -1 to 4095, as said below
Outputs:
- new_history: bfloat16 [128, 4096, 256], P('dom')
- grad_features: bfloat16 [128, 1024, 256], P('dom', 'batch')
- grad_weight: float32 [256, 256], replicated
Inputs may be any that keep to these rules, and one draw needn't show every extreme that they name: `halo_table`: every device's table holds 8 live slots for its own partition and its two neighbours modulo 128; for every other owner at most 2 live slots, exactly 2 for the partition two above its own modulo 128; live slots of an owner come first. `tile_cols`: within each row block the 8 column blocks are distinct, and the first is the row block's own local block. `batch_ids`: live slots come first; live rows are distinct over all batch indices of one partition; in each partition one device has all slots live.
All inputs are finite; a program needn't handle non-finite values.
Results may differ from a plain program's by a relative error of at most 0.011.
Values may be sent and summed in bfloat16 or wider, within the bound.
A program may use at most 64 MiB of HBM per device.

v0:
```python
import math

import jax
import jax.numpy as jnp
from jax import lax
from jax.sharding import PartitionSpec as P

ALPHA_MIX = 0.1
BETA_MIX = math.log(1.5)


def tile_product(tile_vals, picked):
    return jnp.einsum("rkij,rkjh->rih", tile_vals, picked, preferred_element_type=jnp.float32)


def shards(
    features, initial, grad_output, weight, history, halo_table, tile_cols, tile_vals, batch_ids
):
    row_count = features.shape[1]
    feature = features.shape[2]
    tile_size = tile_vals.shape[-1]
    row_blocks = row_count // tile_size
    hist_rows = history.shape[1]
    local_hist = history[0]
    requests = halo_table[0, 0]
    all_ids = batch_ids[0]
    own_ids = lax.dynamic_index_in_dim(all_ids, lax.axis_index("batch"), 0, keepdims=False)
    is_live = (own_ids >= 0)[:, None]
    masked = jnp.where(is_live, features[0], jnp.zeros_like(features[0]))
    local_blocks = masked.reshape(row_blocks, tile_size, feature)
    column_ids = tile_cols[0, 0]
    tile_block = tile_vals[0, 0]
    wanted = lax.all_to_all(requests, "dom", split_axis=0, concat_axis=0, tiled=True)
    fetched = jnp.take(local_hist, jnp.clip(wanted, 0, hist_rows - 1), axis=0)
    fetched_all = lax.all_to_all(
        jnp.where((wanted >= 0)[..., None], fetched, jnp.zeros_like(fetched)),
        "dom",
        split_axis=0,
        concat_axis=0,
        tiled=True,
    )
    blocks = jnp.concatenate([local_blocks, fetched_all.reshape(-1, tile_size, feature)], axis=0)
    picked = jnp.take(blocks, column_ids, axis=0)
    aggregate = tile_product(tile_block, picked).reshape(row_count, feature)
    support = (1.0 - ALPHA_MIX) * aggregate + ALPHA_MIX * initial[0].astype(jnp.float32)
    support_low = support.astype(jnp.bfloat16)
    pre_act = (1.0 - BETA_MIX) * support + BETA_MIX * jnp.dot(
        support_low, weight, preferred_element_type=jnp.float32
    )
    outputs = jax.nn.silu(pre_act).astype(jnp.bfloat16)
    sigmoid_z = jax.nn.sigmoid(pre_act)
    slope = grad_output[0].astype(jnp.float32) * sigmoid_z * (1.0 + pre_act * (1.0 - sigmoid_z))
    grad_pre = jnp.where(is_live, slope, jnp.zeros_like(slope))
    grad_low = grad_pre.astype(jnp.bfloat16)
    grad_w = BETA_MIX * jnp.dot(support_low.T, grad_low, preferred_element_type=jnp.float32)
    devices = lax.axis_size("dom") * lax.axis_size("batch")
    grad_weight = lax.psum(grad_w, ("dom", "batch")) / devices
    grad_sup = (1.0 - BETA_MIX) * grad_pre + BETA_MIX * jnp.dot(
        grad_low, weight.T, preferred_element_type=jnp.float32
    )
    grad_agg = ((1.0 - ALPHA_MIX) * grad_sup).astype(jnp.bfloat16)
    spread = jnp.einsum(
        "rkij,rih->rkjh",
        tile_block,
        grad_agg.reshape(row_blocks, tile_size, feature),
        preferred_element_type=jnp.float32,
    )
    onehot = (
        column_ids[:, :, None] == jnp.arange(row_blocks, dtype=jnp.int32)[None, None, :]
    ).astype(jnp.float32)
    grad_x = jnp.einsum("rkc,rkjh->cjh", onehot, spread).reshape(row_count, feature)
    grad_x = jnp.where(is_live, grad_x, jnp.zeros_like(grad_x)).astype(jnp.bfloat16)
    every = lax.all_gather(outputs[None], "batch", axis=0, tiled=True)
    flat_ids = all_ids.reshape(-1)
    all_target = jnp.where(flat_ids >= 0, flat_ids, hist_rows)
    new_hist = local_hist.at[all_target].set(every.reshape(-1, feature), mode="drop")
    return (new_hist[None], grad_x[None], grad_weight)


def solution(mesh):
    return jax.shard_map(
        shards,
        mesh=mesh,
        in_specs=(
            P("dom", "batch", None),
            P("dom", "batch", None),
            P("dom", "batch", None),
            P(),
            P("dom", None, None),
            P("dom", "batch", None, None),
            P("dom", "batch", None, None),
            P("dom", "batch", None, None, None, None),
            P("dom", None, None),
        ),
        out_specs=(P("dom", None, None), P("dom", "batch", None), P()),
        check_vma=False,
    )
```

profile of v0, /device:TPU:1, one launch (start us, length us, event | category | flops | bytes accessed | tf_op | source)
XLA Modules:
  0.0 552.4 jit_solution(1950462039882178711)
XLA Ops:
  7.2 0.0 copy-start
  7.2 0.0 copy-start.7
  7.2 1.6 copy.35
  8.8 0.0 copy-done.7
  8.8 0.1 copy.21
  8.9 35.2 %all_to_all.14 = s32[128,1,8]{2,1,0:T(1,128)S(1)} all-to-all(s32[128,1,8]{2,1,0:T(1,128)S(1)} %bitcast.88), channel_id=1, replica_groups=mesh['dom'=128,'batch'=4] {'dom'}, dimensions={0} | all-to-all | bytes 8192 | tf_op jit(solution)/shard_map/all_to_all | solution.py:33
  44.3 0.1 copy.23
  44.4 0.1 copy.25
  44.5 0.1 copy.26
  44.6 0.1 reshape.188
  44.7 3.9 gather_fusion
  48.7 0.0 copy-start.8
  48.7 0.0 copy-start.6
  48.7 0.0 copy-start.2
  48.7 1.1 fusion.14
  49.9 6.6 %all-to-all-start.1 = ((bf16[128,8,256]{2,1,0:T(8,128)(2,1)}), bf16[128,8,256]{2,1,0:T(8,128)(2,1)S(1)}, u32[]{:S(2)}, u32[]{:S(2)}) async-start(bf16[128,8,256]{2,1,0:T(8,128)(2,1)} %fusion.14), calls=%async_computation.1 | async-start | bytes 1048576 | tf_op jit(solution)/shard_map/all_to_all | solution.py:35
  56.4 0.0 all-reduce.2.cloned.1.call-start
  56.5 0.0 copy-done.8
  56.5 0.1 reshape.196
  56.6 0.0 copy-done.6
  56.6 0.0 copy-done.2
  56.6 1.2 copy.27
  57.8 0.5 compare_and_fusion.1
  58.4 1.0 broadcast_select_fusion
  59.4 30.4 %all-to-all-done.1 = bf16[128,8,256]{2,1,0:T(8,128)(2,1)S(1)} async-done(((bf16[128,8,256]{2,1,0:T(8,128)(2,1)}), bf16[128,8,256]{2,1,0:T(8,128)(2,1)S(1)}, u32[]{:S(2)}, u32[]{:S(2)}) %all-to-all-start.1) | async-done | bytes 524320 | tf_op jit(solution)/shard_map/all_to_all | solution.py:35
  89.7 0.1 pad_maximum_fusion
  89.8 0.0 copy-start.3
  89.8 0.0 copy-start.5
  89.8 1.6 gather_fusion.1
  91.4 0.0 copy-done.3
  91.4 1.7 fusion.10
  93.1 0.0 copy-done.5
  93.1 0.0 copy-done
  93.2 0.2 multiply_convert_fusion
  93.4 0.0 copy-done.9
  93.4 1.0 convolution_multiply_fusion
  94.4 0.0 copy-start.4
  94.4 0.3 fusion.11
  94.7 0.8 copy-done.4
  95.5 0.6 fusion.7
  96.1 0.0 all-reduce.2.cloned.1.call-update
  96.1 11.8 %all-gather = bf16[1024,256]{1,0:T(8,128)(2,1)S(1)} all-gather(bf16[256,256]{1,0:T(8,128)(2,1)S(1)} %get-tuple-element.3), channel_id=2, replica_groups=mesh['dom'=128,'batch'=4] {'batch'}, dimensions={0}, use_global_device_ids=true | all-gather | bytes 655360 | tf_op jit(solution)/shard_map/all_gather | solution.py:73
  107.9 6.1 %scatter_fusion = bf16[4096,256]{1,0:T(8,128)(2,1)S(1)} fusion(bf16[4096,256]{1,0:T(8,128)(2,1)S(1)} %bitcast.82, s32[1024]{0:T(1024)S(1)} %bitcast.90, bf16[1024,256]{1,0:T(8,128)(2,1)S(1)} %all-gather), kind=kCustom, calls=%fused_computation.2 | custom fusion | bytes 1576960 | tf_op jit(solution)/shard_map/scatter | solution.py:76
  114.0 0.0 copy-start.1
  114.0 0.9 fusion.18
  114.9 428.9 %all-reduce.2.cloned.1.call-done = f32[256,256]{1,0:T(8,128)} async-done(((f32[256,256]{1,0:T(8,128)}), f32[256,256]{1,0:T(8,128)}) %all-reduce.2.cloned.1.call-update) | async-done | bytes 262160 | tf_op jit(solution)/shard_map/psum | solution.py:57
  543.8 1.7 broadcast_multiply_fusion
  545.5 0.0 copy-done.1
  (13 shorter events, 0.2 us)
Async XLA Ops:
  7.2 86.0 %copy-start = (bf16[256,256]{1,0:T(8,128)(2,1)S(1)}, bf16[256,256]{1,0:T(8,128)(2,1)}, u32[]{:S(2)}) copy-start(bf16[256,256]{1,0:T(8,128)(2,1)} %param.12) | copy-start | bytes 393220
  7.2 1.6 copy-start.7
  48.7 7.8 %copy-start.8 = (s32[1,1,2,8]{3,2,1,0:T(2,128)S(1)}, s32[1,1,2,8]{3,2,1,0:T(2,128)}, u32[]{:S(2)}) copy-start(s32[1,1,2,8]{3,2,1,0:T(2,128)} %param.15) | copy-start | bytes 196
  48.7 7.9 %copy-start.6 = (s32[1,4,256]{2,1,0:T(4,128)S(1)}, s32[1,4,256]{2,1,0:T(4,128)}, u32[]{:S(2)}) copy-start(s32[1,4,256]{2,1,0:T(4,128)} %param.17) | copy-start | bytes 12292
  48.7 7.9 %copy-start.2 = (bf16[1,1,2,8,128,128]{5,4,3,2,1,0:T(8,128)(2,1)S(1)}, bf16[1,1,2,8,128,128]{5,4,3,2,1,0:T(8,128)(2,1)}, u32[]{:S(2)}) copy-start(bf16[1,1,2,8,128,128]{5,4,3,2,1,0:T(8,128)(2,1)} %param.16) | copy-start | bytes 1572868
  49.9 39.9 %all-to-all-start.1 = ((bf16[128,8,256]{2,1,0:T(8,128)(2,1)}), bf16[128,8,256]{2,1,0:T(8,128)(2,1)S(1)}, u32[]{:S(2)}, u32[]{:S(2)}) async-start(bf16[128,8,256]{2,1,0:T(8,128)(2,1)} %fusion.14), calls=%async_computation.1 | async-start | bytes 1048576 | tf_op jit(solution)/shard_map/all_to_all | solution.py:35
  56.4 487.4 %all-reduce.2.cloned.1.call-start = ((), (), s32[]{:S(2)}) async-start(), calls=%async_computation.2 | async-start | bytes 524288 | tf_op jit(solution)/shard_map/psum | solution.py:57
  89.8 1.6 copy-start.3
  89.8 3.3 copy-start.5
  91.4 2.0 copy-start.9
  94.4 1.0 copy-start.4
  114.0 431.5 %copy-start.1 = (bf16[4096,256]{1,0:T(8,128)(2,1)}, bf16[4096,256]{1,0:T(8,128)(2,1)S(1)}, u32[]{:S(2)}) copy-start(bf16[4096,256]{1,0:T(8,128)(2,1)S(1)} %scatter_fusion) | copy-start | bytes 6291460
Sparse Core Ops, SparseCore 0:
  96.2 447.5 all-reduce.1
where the time goes:
time: 553 us; the launch traced here: 552 us
  waiting for transfers between devices  459 us (83%)
  blocking collectives  47 us (8%)
  local copies, waits for them, and re-layouts  16 us (3%)
  between operations  14.3 us (3%)
  starting transfers between devices  6.6 us (1%)
    psum x1, waiting for transfers between devices, shards(): grad_weight = lax.psum(grad_w, ('dom', 'batch')) / devices  429 us
    all_to_all x1, blocking collectives, shards(): lax.all_to_all(requests, 'dom', split_axis=0, concat_axis=0, tiled=True)  35.2 us
    all_to_all x1, waiting for transfers between devices, shards(): lax.all_to_all(jnp.where((wanted >= 0)[..., None], fetched, jnp.zeros_lik...  30.4 us
    all_gather x1, blocking collectives, shards(): every = lax.all_gather(outputs[None], 'batch', axis=0, tiled=True)  11.8 us
  transfers between devices with their start and end apart: 2, of which 2 were waited for; matrix products, arithmetic and copies ran while one was open for 2% of the time, Pallas kernels for 0%

commit v1 on v0

v1 whole, which is shorter than its diff:
```python
import math

import jax
import jax.numpy as jnp
from jax import lax
from jax.experimental import pallas as pl
from jax.experimental.pallas import tpu as pltpu
from jax.sharding import PartitionSpec as P

ALPHA_MIX = 0.1
BETA_MIX = math.log(1.5)
X, Z, C, Y = 4, 16, 2, 4
N_DOM = X * Z * C
GROUP = X * Y * C
H = 256
TILE = 128
ROWS = 256
HIST = 4096
CAP = 8
K = 8
NB = 2 + N_DOM * CAP // TILE
PART = Y * ROWS
BASE = 8192
CHUNK = 512
BF = jnp.bfloat16
F32 = jnp.float32
I32 = jnp.int32


def coords():
    d = lax.axis_index("dom")
    return lax.div(d, Z * C), lax.rem(lax.div(d, C), Z), lax.rem(d, C), lax.axis_index("batch")


def dom_of(x, z, c):
    return (x * Z + z) * C + c


def each_dom_peer(fn):
    x, z, c, _ = coords()

    def plane(zz, own):
        for dx in (2, 1, 3, 0):
            for dc in (1, 0):
                if not (own and dx == 0 and dc == 0):
                    fn(dom_of(lax.rem(x + dx, X), zz, lax.rem(c + dc, C)))

    def body(k, carry):
        odd, half = lax.rem(k, 2), lax.div(k, 2)
        plane(lax.rem(z + Z // 2 + half * (1 - 2 * odd) - odd, Z), False)
        return carry

    lax.fori_loop(0, Z - 1, body, 0)
    plane(z, True)


def group_peers(skip_same_batch):
    x, z, c, b = coords()
    out = []
    for dx in (2, 1, 3, 0):
        for dy in (2, 1, 3, 0):
            for dc in (1, 0):
                if (dx, dy, dc) == (0, 0, 0) or (skip_same_batch and dy == 0):
                    continue
                qx, qy, qc = lax.rem(x + dx, X), lax.rem(b + dy, Y), lax.rem(c + dc, C)
                out.append(((qx * Y + qy) * C + qc, {"dom": dom_of(qx, z, qc), "batch": qy}))
    return out


def z_peers():
    x, z, c, _ = coords()
    return [{"dom": dom_of(x, lax.rem(z + i, Z), c)} for i in (8, 7, 9, 6, 10, 5, 11, 4, 12, 3, 13, 2, 14, 1, 15)]


def remote(src, dst, send, recv, device):
    return pltpu.make_async_remote_copy(src_ref=src, dst_ref=dst, send_sem=send, recv_sem=recv, device_id=device)


def wait_bytes(like, sem):
    pltpu.make_async_copy(like, like, sem).wait()


def iota(shape, dim):
    return lax.broadcasted_iota(I32, shape, dim)


def ones_where(mask):
    return jnp.where(mask, 1.0, 0.0).astype(BF)


def mm(a, b, dims=((1,), (0,))):
    return lax.dot_general(a, b, (dims, ((), ())), preferred_element_type=F32)


def kernel(
    tab_h, ids_h, cols_h, hist_h, feat_h, init_h, gout_h, w_h, tiles_h,
    nh_o, gx_o, gw_o,
    tab, ids, cols, hist, feat, init, gout, w, tiles,
    req, wreq, ntab, sbuf, rbuf, nsend, nrow, perm, e_lo, e_hi, e_near, place, blocks, live,
    outs, gsend, grecv, zsend, zrecv, asend, arecv,
    in_sem, req_s, req_r, nreq_s, nreq_r, row_s, row_r, nrow_s, nrow_r, rs_s, rs_r, z_s, z_r, ag_s, ag_r, y_s, y_r, out_sem,
):
    x, z, c, b = coords()
    me = lax.axis_index("dom")
    pairs = [
        (tab_h, tab), (ids_h, ids), (cols_h, cols), (hist_h, hist), (feat_h, feat),
        (init_h, init), (gout_h, gout), (w_h, w), (tiles_h, tiles),
    ]
    loads = [pltpu.make_async_copy(src, dst, in_sem.at[i]) for i, (src, dst) in enumerate(pairs)]
    for load in loads:
        load.start()

    barrier = pltpu.get_barrier_semaphore()
    each_dom_peer(lambda p: pl.semaphore_signal(barrier, inc=1, device_id={"dom": p}))
    others = group_peers(True)
    for _, device in others:
        pl.semaphore_signal(barrier, inc=1, device_id=device)

    loads[0].wait()
    req[...] = (tab[0:1, :] + 1) * BASE + (tab[1:2, :] + 1)
    wreq[pl.ds(me, 1)] = jnp.zeros((1, 1, N_DOM), I32)
    right, left = lax.rem(me + 1, N_DOM), lax.rem(me + N_DOM - 1, N_DOM)
    pl.semaphore_wait(barrier, N_DOM - 1 + len(others))
    near_req = [remote(tab, ntab.at[i], nreq_s.at[i], nreq_r.at[i], {"dom": p}) for i, p in enumerate((right, left))]
    for copy in near_req:
        copy.start()
    each_dom_peer(lambda p: remote(req, wreq.at[me], req_s, req_r, {"dom": p}).start())

    loads[1].wait()

    def place_chunk(i, carry):
        rows = iota((CHUNK, ROWS), 0) + i * CHUNK
        for q in range(Y):
            place[pl.ds(pl.multiple_of(i * CHUNK, CHUNK), CHUNK), pl.ds(q * ROWS, ROWS)] = ones_where(rows == ids[q : q + 1, :])
        return carry

    lax.fori_loop(0, HIST // CHUNK, place_chunk, 0)
    r4 = iota((4 * N_DOM, 2 * N_DOM), 0)
    pick = lax.rem(r4, 4) // 2 * N_DOM + r4 // 4 == iota((4 * N_DOM, 2 * N_DOM), 1)
    perm[:, 0 : 2 * N_DOM] = ones_where(pick & (lax.rem(r4, 2) == 0))
    perm[:, 2 * N_DOM :] = ones_where(pick & (lax.rem(r4, 2) == 1))
    loads[3].wait()

    wait_bytes(wreq.at[pl.ds(0, N_DOM - 1)], req_r)
    for copy in near_req:
        copy.wait_recv()

    lane_me = iota((1, N_DOM), 1) == me

    def column(v):
        return jnp.sum(jnp.where(lane_me, v.astype(F32), 0.0), axis=1, keepdims=True)

    asked = wreq[...].reshape(N_DOM, N_DOM)
    wanted = jnp.concatenate(
        [
            column(lax.shift_right_logical(asked, 13) - 1),
            column(jnp.bitwise_and(asked, BASE - 1) - 1),
            column(tab[...]),
            column(ntab[0]),
            column(ntab[1]),
            jnp.full((8, 1), -1.0, F32),
        ],
        axis=0,
    ).astype(I32)
    n_ask = 2 * N_DOM + 32
    got = jnp.zeros((n_ask, H), F32)
    for i in range(HIST // CHUNK):
        hot = ones_where(wanted == iota((n_ask, CHUNK), 1) + i * CHUNK)
        got = got + mm(hot, hist[pl.ds(i * CHUNK, CHUNK), :])
    n0 = 2 * N_DOM
    nsend[0] = got[n0 + 16 : n0 + 24, :].astype(BF)
    nsend[1] = got[n0 + 8 : n0 + 16, :].astype(BF)
    near_row = [remote(nsend.at[i], nrow.at[i], nrow_s.at[i], nrow_r.at[i], {"dom": p}) for i, p in enumerate((right, left))]
    for copy in near_row:
        copy.start()
    far = got[0:n0, :].astype(BF)
    halves = jnp.concatenate([far[:, 0:TILE], far[:, TILE:]], axis=0)
    sbuf[...] = mm(perm[...], halves).astype(BF).reshape(N_DOM, 4, TILE)
    rbuf[pl.ds(me, 1)] = jnp.zeros((1, 4, TILE), BF)
    each_dom_peer(lambda p: remote(sbuf.at[p], rbuf.at[me], row_s, row_r, {"dom": p}).start())

    own_rows = got[n0 : n0 + 8, :]
    shape = (N_DOM * CAP, 4 * N_DOM)
    p_row, p_col = iota(shape, 0), iota(shape, 1)
    slot = lax.rem(p_row, CAP)
    spot = jnp.where(slot < 2, p_row // CAP * 4 + slot * 2, -8)
    e_lo[...] = ones_where(p_col == spot)
    e_hi[...] = ones_where(p_col == spot + 1)
    shape = (N_DOM * CAP, 32)
    p_row, p_col = iota(shape, 0), iota(shape, 1)
    who, slot = p_col // 8, lax.rem(p_col, 8)
    owner = jnp.where(who == 0, me, jnp.where(who == 1, left, right))
    e_near[...] = ones_where((p_row == owner * CAP + slot) & (who < 3) & ((who == 0) | (slot >= 2)))
    mine = jnp.sum(jnp.where(iota((Y, ROWS), 0) == b, (ids[...] >= 0).astype(F32), 0.0), axis=0, keepdims=True)
    live_col = jnp.sum(jnp.where(iota((ROWS, ROWS), 0) == iota((ROWS, ROWS), 1), mine, 0.0), axis=1, keepdims=True)
    live[...] = jnp.broadcast_to(live_col, (ROWS, H))
    loads[4].wait()
    masked = jnp.where(live[...] > 0, feat[...].astype(F32), 0.0).astype(BF)
    blocks[0:2] = masked.reshape(2, TILE, H)

    def clear_chunk(i, carry):
        rows = pl.ds(pl.multiple_of(i * CHUNK, CHUNK), CHUNK)
        hit = jnp.max(place[rows, :].astype(F32), axis=1, keepdims=True)
        hist[rows, :] = jnp.where(hit > 0, 0.0, hist[rows, :].astype(F32)).astype(BF)
        return carry

    lax.fori_loop(0, HIST // CHUNK, clear_chunk, 0)
    for load in (loads[2], *loads[5:]):
        load.wait()

    for copy in near_row:
        copy.wait_recv()
    wait_bytes(rbuf.at[pl.ds(0, N_DOM - 1)], row_r)

    near = jnp.concatenate([own_rows, nrow[0].astype(F32), nrow[1].astype(F32), jnp.zeros((8, H), F32)], axis=0).astype(BF)
    near = mm(e_near[...], near)
    came = rbuf[...].reshape(4 * N_DOM, TILE)
    blocks[2:NB, :, 0:TILE] = (mm(e_lo[...], came) + near[:, 0:TILE]).astype(BF).reshape(NB - 2, TILE, TILE)
    blocks[2:NB, :, TILE:] = (mm(e_hi[...], came) + near[:, TILE:]).astype(BF).reshape(NB - 2, TILE, TILE)

    agg = []
    for r in range(2):
        total = None
        for k in range(0, K, 2):
            lhs = jnp.concatenate([tiles[r, k], tiles[r, k + 1]], axis=1)
            rhs = jnp.concatenate([blocks[cols[r, k]], blocks[cols[r, k + 1]]], axis=0)
            term = mm(lhs, rhs)
            total = term if total is None else total + term
        agg.append(total)
    support = (1.0 - ALPHA_MIX) * jnp.concatenate(agg, axis=0) + ALPHA_MIX * init[...].astype(F32)
    support_low = support.astype(BF)
    pre_act = (1.0 - BETA_MIX) * support + BETA_MIX * mm(support_low, w[...])
    sig = jax.nn.sigmoid(pre_act)
    slope = gout[...].astype(F32) * sig * (1.0 + pre_act * (1.0 - sig))
    grad_pre = jnp.where(live[...] > 0, slope, 0.0)
    grad_low = grad_pre.astype(BF)
    grad_w = mm(support_low, grad_low, ((0,), (0,)))

    gsend[...] = grad_w.astype(BF).reshape(GROUP, H // GROUP, H)
    slice_me = (x * Y + b) * C + c
    peers = group_peers(False)
    for slot_q, device in peers:
        remote(gsend.at[slot_q], grecv.at[slice_me], rs_s, rs_r, device).start()
    outs[pl.ds(b, 1)] = (pre_act * sig).astype(BF).reshape(1, ROWS, H)
    y_right, y_left = {"batch": lax.rem(b + 1, Y)}, {"batch": lax.rem(b + Y - 1, Y)}
    ring = [remote(outs.at[b], outs.at[b], y_s.at[i], y_r.at[i], p) for i, p in enumerate((y_right, y_left))]
    for copy in ring:
        copy.start()
    grecv[pl.ds(slice_me, 1)] = gsend[pl.ds(slice_me, 1)]

    grad_sup = (1.0 - BETA_MIX) * grad_pre + BETA_MIX * mm(grad_low, w[...], ((1,), (1,)))
    grad_agg = ((1.0 - ALPHA_MIX) * grad_sup).astype(BF)
    g = [grad_agg[0:TILE, :], grad_agg[TILE:, :]]
    for q in range(2):
        total = mm(tiles[q, 0], g[q], ((0,), (0,)))
        at, found = jnp.int32(0), jnp.int32(0)
        for k in range(1, K):
            same = cols[1 - q, k] == q
            at, found = jnp.where(same, k, at), jnp.where(same, 1, found)
        other = jnp.where(jnp.full((TILE, TILE), found, I32) > 0, tiles[1 - q, at].astype(F32), 0.0).astype(BF)
        total = total + mm(other, g[1 - q], ((0,), (0,)))
        rows = slice(q * TILE, (q + 1) * TILE)
        gx_o[rows, :] = jnp.where(live[rows, :] > 0, total, 0.0).astype(BF)

    wait_bytes(grecv.at[pl.ds(0, GROUP - 1)], rs_r)
    zsend[...] = jnp.sum(grecv[...].astype(F32), axis=0).astype(BF)
    for device in z_peers():
        remote(zsend, zrecv.at[z], z_s, z_r, device).start()
    zrecv[pl.ds(z, 1)] = zsend[...].reshape(1, H // GROUP, H)

    half = ROWS // 2
    ring[0].wait_recv()
    before, after = lax.rem(b + Y - 1, Y), lax.rem(b + 1, Y)
    on = [
        remote(outs.at[before, pl.ds(0, half)], outs.at[before, pl.ds(0, half)], y_s.at[2], y_r.at[2], y_right),
        remote(outs.at[after, pl.ds(half, half)], outs.at[after, pl.ds(half, half)], y_s.at[3], y_r.at[3], y_left),
    ]
    on[0].start()
    ring[1].wait_recv()
    on[1].start()
    for copy in on:
        copy.wait_recv()

    stores = []

    def scatter(i):
        rows = pl.ds(i * CHUNK, CHUNK)
        new = hist[rows, :].astype(F32) + mm(place[rows, :], outs[...].reshape(PART, H))
        hist[rows, :] = new.astype(BF)
        store = pltpu.make_async_copy(hist.at[rows], nh_o.at[rows], out_sem.at[i])
        store.start()
        stores.append(store)

    for i in range(4):
        scatter(i)
    wait_bytes(zrecv.at[pl.ds(0, Z - 1)], z_r)
    scale = BETA_MIX / (N_DOM * Y)
    asend[...] = (scale * jnp.sum(zrecv[...].astype(F32), axis=0)).astype(BF)
    for _, device in peers:
        remote(asend, arecv.at[slice_me], ag_s, ag_r, device).start()
    arecv[pl.ds(slice_me, 1)] = asend[...].reshape(1, H // GROUP, H)
    for i in range(4, HIST // CHUNK):
        scatter(i)

    for copy in near_req + near_row + ring + on:
        copy.wait_send()
    wait_bytes(wreq.at[pl.ds(0, N_DOM - 1)], req_s)
    wait_bytes(rbuf.at[pl.ds(0, N_DOM - 1)], row_s)
    wait_bytes(grecv.at[pl.ds(0, GROUP - 1)], rs_s)
    wait_bytes(zrecv.at[pl.ds(0, Z - 1)], z_s)
    wait_bytes(arecv.at[pl.ds(0, GROUP - 1)], ag_s)
    for store in stores:
        store.wait()
    wait_bytes(arecv.at[pl.ds(0, GROUP - 1)], ag_r)
    gw_o[...] = arecv[...].astype(F32).reshape(H, H)


def hand_on(nh_i, gx_i, gw_i, nh_o, gx_o, gw_o, nh, gx, gw, sem_in, sem_out):
    parts = [(nh_i.at[pl.ds(i * 1024, 1024)], nh.at[pl.ds(i * 1024, 1024)], nh_o.at[pl.ds(i * 1024, 1024)]) for i in range(4)]
    parts = [(gw_i, gw, gw_o), (gx_i, gx, gx_o), *parts]
    come = [pltpu.make_async_copy(src, mid, sem_in.at[i]) for i, (src, mid, _) in enumerate(parts)]
    go = [pltpu.make_async_copy(mid, dst, sem_out.at[i]) for i, (_, mid, dst) in enumerate(parts)]
    for copy in come:
        copy.start()
    for first, then in zip(come, go):
        first.wait()
        then.start()
    for copy in go:
        copy.wait()


def shards(features, initial, grad_output, weight, history, halo_table, tile_cols, tile_vals, batch_ids):
    hbm = pl.BlockSpec(memory_space=pl.ANY)
    vmem = pl.BlockSpec(memory_space=pltpu.VMEM)
    v = pltpu.VMEM
    dma = pltpu.SemaphoreType.DMA
    table = jnp.transpose(halo_table[0, 0])
    shapes = (
        jax.ShapeDtypeStruct((HIST, H), BF),
        jax.ShapeDtypeStruct((ROWS, H), BF),
        jax.ShapeDtypeStruct((H, H), F32),
    )
    piece = H // GROUP
    parts = pl.pallas_call(
        kernel,
        out_shape=shapes,
        in_specs=[hbm] * 9,
        out_specs=(hbm, vmem, vmem),
        scratch_shapes=[
            v((CAP, N_DOM), I32), v((Y, ROWS), I32), pltpu.SMEM((2, K), I32), v((HIST, H), BF), v((ROWS, H), BF),
            v((ROWS, H), BF), v((ROWS, H), BF), v((H, H), BF), v((2, K, TILE, TILE), BF),
            v((1, N_DOM), I32), v((N_DOM, 1, N_DOM), I32), v((2, CAP, N_DOM), I32),
            v((N_DOM, 4, TILE), BF), v((N_DOM, 4, TILE), BF), v((2, CAP, H), BF), v((2, CAP, H), BF),
            v((4 * N_DOM, 4 * N_DOM), BF), v((N_DOM * CAP, 4 * N_DOM), BF), v((N_DOM * CAP, 4 * N_DOM), BF),
            v((N_DOM * CAP, 32), BF), v((HIST, PART), BF), v((NB, TILE, H), BF), v((ROWS, H), F32),
            v((Y, ROWS, H), BF), v((GROUP, piece, H), BF), v((GROUP, piece, H), BF), v((piece, H), BF),
            v((Z, piece, H), BF), v((piece, H), BF), v((GROUP, piece, H), BF),
            dma((9,)), dma(()), dma(()), dma((2,)), dma((2,)), dma(()), dma(()), dma((2,)), dma((2,)),
            dma(()), dma(()), dma(()), dma(()), dma(()), dma(()), dma((4,)), dma((4,)), dma((HIST // CHUNK,)),
        ],
        compiler_params=pltpu.CompilerParams(collective_id=0, has_side_effects=True, vmem_limit_bytes=60 * 1024 * 1024),
        name="layer",
    )(table, batch_ids[0], tile_cols[0, 0], history[0], features[0], initial[0], grad_output[0], weight, tile_vals[0, 0])
    new_hist, grad_x, grad_w = pl.pallas_call(
        hand_on,
        out_shape=shapes,
        in_specs=[hbm] * 3,
        out_specs=(hbm, hbm, hbm),
        scratch_shapes=[v((HIST, H), BF), v((ROWS, H), BF), v((H, H), F32), dma((6,)), dma((6,))],
        compiler_params=pltpu.CompilerParams(vmem_limit_bytes=60 * 1024 * 1024),
        name="hand_on",
    )(*parts)
    return new_hist[None], grad_x[None], grad_w


def solution(mesh):
    return jax.shard_map(
        shards,
        mesh=mesh,
        in_specs=(
            P("dom", "batch", None),
            P("dom", "batch", None),
            P("dom", "batch", None),
            P(),
            P("dom", None, None),
            P("dom", "batch", None, None),
            P("dom", "batch", None, None),
            P("dom", "batch", None, None, None, None),
            P("dom", None, None),
        ),
        out_specs=(P("dom", None, None), P("dom", "batch", None), P()),
        check_vma=False,
    )
```

time: 553 us -> 61.7 us (0.11)
  waiting for transfers between devices: 459 us -> 0 us
  Pallas kernels: 0 us -> 60.9 us
  blocking collectives: 47 us -> 0 us
  local copies, waits for them, and re-layouts: 16 us -> 0 us
  between operations: 14.3 us -> 0.64 us
  starting transfers between devices: 6.6 us -> 0 us
    psum x1 -> x0, waiting for transfers between devices: 429 us -> none  [shards(): grad_weight = lax.psum(grad_w, ('dom', 'batch')) / devices]
    pallas_call x0 -> x2, Pallas kernels: none -> 60.9 us  [the longest x1 58.3 us: shards(): pl.pallas_call(kernel, out_shape=shapes, in_specs=[hbm] * 9, out_specs=(h...]
    all_to_all x1 -> x0, blocking collectives: 35.2 us -> none  [shards(): lax.all_to_all(requests, 'dom', split_axis=0, concat_axis=0, tiled=True)]
    all_to_all x1 -> x0, waiting for transfers between devices: 30.4 us -> none  [shards(): lax.all_to_all(jnp.where((wanted >= 0)[..., None], fetched, jnp.zeros_lik...]
    all_gather x1 -> x0, blocking collectives: 11.8 us -> none  [shards(): every = lax.all_gather(outputs[None], 'batch', axis=0, tiled=True)]
    all_to_all x1 -> x0, starting transfers between devices: 6.56 us -> none  [shards(): lax.all_to_all(jnp.where((wanted >= 0)[..., None], fetched, jnp.zeros_lik...]
    scatter x1 -> x0, local copies, waits for them, and re-layouts: 6.1 us -> none  [shards(): local_hist.at[all_target].set(every.reshape(-1, feature), mode='drop')]
  transfers between devices with their start and end apart: 2 -> 0, of which waited for: 2 -> 0; matrix products, arithmetic and copies ran while one was open for 2% -> 0% of each run, Pallas kernels for 0% -> 0%
where the time goes in v1:
time: 61.7 us; the launch traced here: 61.6 us
  Pallas kernels  60.9 us (99%)
  between operations  0.64 us (1%)
    pallas_call x1, Pallas kernels, shards(): pl.pallas_call(kernel, out_shape=shapes, in_specs=[hbm] * 9, out_specs=(h...  58.3 us
    pallas_call x1, Pallas kernels, shards(): pl.pallas_call(hand_on, out_shape=shapes, in_specs=[hbm] * 3, out_specs=(...  2.6 us

profile of v1, /device:TPU:1, one launch (start us, length us, event | category | flops | bytes accessed | tf_op | source)
XLA Modules:
  0.0 61.6 jit_solution(2372479471553535575)
XLA Ops:
  0.6 58.3 %layer.1 = (bf16[4096,256]{1,0:T(8,128)(2,1)}, bf16[256,256]{1,0:T(8,128)(2,1)}, f32[256,256]{1,0:T(8,128)}) custom-call(s32[8,128]{1,0:T(8,128)} %bitcast.17, s32[4,256]{1,0:T(4,128)} %bitcast.18, s32[2,8]{1,0:T(2,128)} %bitcast.19, bf16[4096,256]{1,0:T(8,128)(2,1)} %bitcast.12, bf16[256,256]{1,0:T(8,128)(2,1)} %bitcast.14, bf16[256,256]{1,0:T(8,128)(2,1)} %bitcast.15, ...), custom_call_target="tpu_custom_call" | custom-call | tf_op jit(solution)/shard_map/layer/pallas_call | solution.py:344
  59.0 2.6 %hand_on.1 = (bf16[4096,256]{1,0:T(8,128)(2,1)}, bf16[256,256]{1,0:T(8,128)(2,1)}, f32[256,256]{1,0:T(8,128)}) custom-call(bf16[4096,256]{1,0:T(8,128)(2,1)} %get-tuple-element.9.nh_i, bf16[256,256]{1,0:T(8,128)(2,1)} %get-tuple-element.10.gx_i, f32[256,256]{1,0:T(8,128)} %get-tuple-element.11.gw_i), custom_call_target="tpu_custom_call" | custom-call | tf_op jit(solution)/shard_map/hand_on/pallas_call | solution.py:364

commit v2 on v1

--- a/solution.py
+++ b/solution.py
@@ -96,9 +96,9 @@
     tab_h, ids_h, cols_h, hist_h, feat_h, init_h, gout_h, w_h, tiles_h,
     nh_o, gx_o, gw_o,
     tab, ids, cols, hist, feat, init, gout, w, tiles,
-    req, wreq, ntab, sbuf, rbuf, nsend, nrow, perm, e_lo, e_hi, e_near, place, blocks, live,
+    req, wreq, ntab, mixed, sbuf, rbuf, nsend, nrow, adj, adj_far, adj_near, place, base, live,
     outs, gsend, grecv, zsend, zrecv, asend, arecv,
-    in_sem, req_s, req_r, nreq_s, nreq_r, row_s, row_r, nrow_s, nrow_r, rs_s, rs_r, z_s, z_r, ag_s, ag_r, y_s, y_r, out_sem,
+    in_sem, req_s, req_r, nreq_s, nreq_r, row_s, row_r, nrow_s, nrow_r, rs_s, rs_r, z_s, z_r, ag_s, ag_r, y_s, y_r,
 ):
     x, z, c, b = coords()
     me = lax.axis_index("dom")
@@ -107,14 +107,14 @@
         (init_h, init), (gout_h, gout), (w_h, w), (tiles_h, tiles),
     ]
     loads = [pltpu.make_async_copy(src, dst, in_sem.at[i]) for i, (src, dst) in enumerate(pairs)]
-    for load in loads:
-        load.start()
-
+    loads[0].start()
     barrier = pltpu.get_barrier_semaphore()
     each_dom_peer(lambda p: pl.semaphore_signal(barrier, inc=1, device_id={"dom": p}))
     others = group_peers(True)
     for _, device in others:
         pl.semaphore_signal(barrier, inc=1, device_id=device)
+    for load in loads[1:]:
+        load.start()
 
     loads[0].wait()
     req[...] = (tab[0:1, :] + 1) * BASE + (tab[1:2, :] + 1)
@@ -135,10 +135,6 @@
         return carry
 
     lax.fori_loop(0, HIST // CHUNK, place_chunk, 0)
-    r4 = iota((4 * N_DOM, 2 * N_DOM), 0)
-    pick = lax.rem(r4, 4) // 2 * N_DOM + r4 // 4 == iota((4 * N_DOM, 2 * N_DOM), 1)
-    perm[:, 0 : 2 * N_DOM] = ones_where(pick & (lax.rem(r4, 2) == 0))
-    perm[:, 2 * N_DOM :] = ones_where(pick & (lax.rem(r4, 2) == 1))
     loads[3].wait()
 
     wait_bytes(wreq.at[pl.ds(0, N_DOM - 1)], req_r)
@@ -173,61 +169,63 @@
     near_row = [remote(nsend.at[i], nrow.at[i], nrow_s.at[i], nrow_r.at[i], {"dom": p}) for i, p in enumerate((right, left))]
     for copy in near_row:
         copy.start()
-    far = got[0:n0, :].astype(BF)
-    halves = jnp.concatenate([far[:, 0:TILE], far[:, TILE:]], axis=0)
-    sbuf[...] = mm(perm[...], halves).astype(BF).reshape(N_DOM, 4, TILE)
-    rbuf[pl.ds(me, 1)] = jnp.zeros((1, 4, TILE), BF)
+    for i in range(2):
+        for j in range(2):
+            mixed[j, pl.ds(i, N_DOM, 2), :] = got[i * N_DOM : (i + 1) * N_DOM, j * TILE : (j + 1) * TILE]
+    sbuf[...] = jnp.concatenate([mixed[0], mixed[1]], axis=1).astype(BF).reshape(N_DOM, 2, H)
+    rbuf[pl.ds(me, 1)] = jnp.zeros((1, 2, H), BF)
     each_dom_peer(lambda p: remote(sbuf.at[p], rbuf.at[me], row_s, row_r, {"dom": p}).start())
 
     own_rows = got[n0 : n0 + 8, :]
-    shape = (N_DOM * CAP, 4 * N_DOM)
+    for i in (2, 8):
+        loads[i].wait()
+    for r in range(2):
+        for col in range(NB):
+            at, found = jnp.int32(0), jnp.int32(1 if col == r else 0)
+            for k in range(1, K if col != r else 1):
+                same = cols[r, k] == col
+                at, found = jnp.where(same, k, at), jnp.where(same, 1, found)
+            tile = tiles[r, at]
+            if col != r:
+                tile = jnp.where(jnp.full((TILE, TILE), found, I32) > 0, tile.astype(F32), 0.0).astype(BF)
+            adj[r * TILE : (r + 1) * TILE, col * TILE : (col + 1) * TILE] = tile
+    shape = (N_DOM * CAP, 2 * N_DOM)
     p_row, p_col = iota(shape, 0), iota(shape, 1)
     slot = lax.rem(p_row, CAP)
-    spot = jnp.where(slot < 2, p_row // CAP * 4 + slot * 2, -8)
-    e_lo[...] = ones_where(p_col == spot)
-    e_hi[...] = ones_where(p_col == spot + 1)
+    spread = ones_where(p_col == jnp.where(slot < 2, p_row // CAP * 2 + slot, -1))
+    adj_far[...] = mm(adj[:, 2 * TILE :], spread).astype(BF)
     shape = (N_DOM * CAP, 32)
     p_row, p_col = iota(shape, 0), iota(shape, 1)
     who, slot = p_col // 8, lax.rem(p_col, 8)
     owner = jnp.where(who == 0, me, jnp.where(who == 1, left, right))
-    e_near[...] = ones_where((p_row == owner * CAP + slot) & (who < 3) & ((who == 0) | (slot >= 2)))
+    spread = ones_where((p_row == owner * CAP + slot) & (who < 3) & ((who == 0) | (slot >= 2)))
+    adj_near[...] = mm(adj[:, 2 * TILE :], spread).astype(BF)
     mine = jnp.sum(jnp.where(iota((Y, ROWS), 0) == b, (ids[...] >= 0).astype(F32), 0.0), axis=0, keepdims=True)
     live_col = jnp.sum(jnp.where(iota((ROWS, ROWS), 0) == iota((ROWS, ROWS), 1), mine, 0.0), axis=1, keepdims=True)
     live[...] = jnp.broadcast_to(live_col, (ROWS, H))
     loads[4].wait()
+    loads[5].wait()
     masked = jnp.where(live[...] > 0, feat[...].astype(F32), 0.0).astype(BF)
-    blocks[0:2] = masked.reshape(2, TILE, H)
+    base[...] = (1.0 - ALPHA_MIX) * mm(adj[:, 0 : 2 * TILE], masked) + ALPHA_MIX * init[...].astype(F32)
 
     def clear_chunk(i, carry):
         rows = pl.ds(pl.multiple_of(i * CHUNK, CHUNK), CHUNK)
         hit = jnp.max(place[rows, :].astype(F32), axis=1, keepdims=True)
-        hist[rows, :] = jnp.where(hit > 0, 0.0, hist[rows, :].astype(F32)).astype(BF)
+        nh_o[rows, :] = jnp.where(hit > 0, 0.0, hist[rows, :].astype(F32)).astype(BF)
         return carry
 
     lax.fori_loop(0, HIST // CHUNK, clear_chunk, 0)
-    for load in (loads[2], *loads[5:]):
-        load.wait()
+    for i in (6, 7):
+        loads[i].wait()
 
     for copy in near_row:
         copy.wait_recv()
     wait_bytes(rbuf.at[pl.ds(0, N_DOM - 1)], row_r)
 
     near = jnp.concatenate([own_rows, nrow[0].astype(F32), nrow[1].astype(F32), jnp.zeros((8, H), F32)], axis=0).astype(BF)
-    near = mm(e_near[...], near)
-    came = rbuf[...].reshape(4 * N_DOM, TILE)
-    blocks[2:NB, :, 0:TILE] = (mm(e_lo[...], came) + near[:, 0:TILE]).astype(BF).reshape(NB - 2, TILE, TILE)
-    blocks[2:NB, :, TILE:] = (mm(e_hi[...], came) + near[:, TILE:]).astype(BF).reshape(NB - 2, TILE, TILE)
-
-    agg = []
-    for r in range(2):
-        total = None
-        for k in range(0, K, 2):
-            lhs = jnp.concatenate([tiles[r, k], tiles[r, k + 1]], axis=1)
-            rhs = jnp.concatenate([blocks[cols[r, k]], blocks[cols[r, k + 1]]], axis=0)
-            term = mm(lhs, rhs)
-            total = term if total is None else total + term
-        agg.append(total)
-    support = (1.0 - ALPHA_MIX) * jnp.concatenate(agg, axis=0) + ALPHA_MIX * init[...].astype(F32)
+
+    halo = mm(adj_far[...], rbuf[...].reshape(2 * N_DOM, H)) + mm(adj_near[...], near)
+    support = base[...] + (1.0 - ALPHA_MIX) * halo
     support_low = support.astype(BF)
     pre_act = (1.0 - BETA_MIX) * support + BETA_MIX * mm(support_low, w[...])
     sig = jax.nn.sigmoid(pre_act)
@@ -242,25 +240,12 @@
     for slot_q, device in peers:
         remote(gsend.at[slot_q], grecv.at[slice_me], rs_s, rs_r, device).start()
     outs[pl.ds(b, 1)] = (pre_act * sig).astype(BF).reshape(1, ROWS, H)
-    y_right, y_left = {"batch": lax.rem(b + 1, Y)}, {"batch": lax.rem(b + Y - 1, Y)}
-    ring = [remote(outs.at[b], outs.at[b], y_s.at[i], y_r.at[i], p) for i, p in enumerate((y_right, y_left))]
-    for copy in ring:
-        copy.start()
     grecv[pl.ds(slice_me, 1)] = gsend[pl.ds(slice_me, 1)]
 
     grad_sup = (1.0 - BETA_MIX) * grad_pre + BETA_MIX * mm(grad_low, w[...], ((1,), (1,)))
     grad_agg = ((1.0 - ALPHA_MIX) * grad_sup).astype(BF)
-    g = [grad_agg[0:TILE, :], grad_agg[TILE:, :]]
-    for q in range(2):
-        total = mm(tiles[q, 0], g[q], ((0,), (0,)))
-        at, found = jnp.int32(0), jnp.int32(0)
-        for k in range(1, K):
-            same = cols[1 - q, k] == q
-            at, found = jnp.where(same, k, at), jnp.where(same, 1, found)
-        other = jnp.where(jnp.full((TILE, TILE), found, I32) > 0, tiles[1 - q, at].astype(F32), 0.0).astype(BF)
-        total = total + mm(other, g[1 - q], ((0,), (0,)))
-        rows = slice(q * TILE, (q + 1) * TILE)
-        gx_o[rows, :] = jnp.where(live[rows, :] > 0, total, 0.0).astype(BF)
+    grad_x = mm(adj[:, 0 : 2 * TILE], grad_agg, ((0,), (0,)))
+    gx_o[...] = jnp.where(live[...] > 0, grad_x, 0.0).astype(BF)
 
     wait_bytes(grecv.at[pl.ds(0, GROUP - 1)], rs_r)
     zsend[...] = jnp.sum(grecv[...].astype(F32), axis=0).astype(BF)
@@ -268,39 +253,39 @@
         remote(zsend, zrecv.at[z], z_s, z_r, device).start()
     zrecv[pl.ds(z, 1)] = zsend[...].reshape(1, H // GROUP, H)
 
+    y_right, y_left = {"batch": lax.rem(b + 1, Y)}, {"batch": lax.rem(b + Y - 1, Y)}
+    ring = [remote(outs.at[b], outs.at[b], y_s.at[i], y_r.at[i], p) for i, p in enumerate((y_right, y_left))]
+    for copy in ring:
+        copy.start()
+
+    def scatter(q):
+        lanes = pl.ds(pl.multiple_of(q * ROWS, ROWS), ROWS)
+        for i in range(HIST // CHUNK):
+            rows = pl.ds(i * CHUNK, CHUNK)
+            nh_o[rows, :] = (nh_o[rows, :].astype(F32) + mm(place[rows, lanes], outs[q])).astype(BF)
+
+    scatter(b)
     half = ROWS // 2
-    ring[0].wait_recv()
     before, after = lax.rem(b + Y - 1, Y), lax.rem(b + 1, Y)
     on = [
         remote(outs.at[before, pl.ds(0, half)], outs.at[before, pl.ds(0, half)], y_s.at[2], y_r.at[2], y_right),
         remote(outs.at[after, pl.ds(half, half)], outs.at[after, pl.ds(half, half)], y_s.at[3], y_r.at[3], y_left),
     ]
+    ring[0].wait_recv()
     on[0].start()
     ring[1].wait_recv()
     on[1].start()
-    for copy in on:
-        copy.wait_recv()
-
-    stores = []
-
-    def scatter(i):
-        rows = pl.ds(i * CHUNK, CHUNK)
-        new = hist[rows, :].astype(F32) + mm(place[rows, :], outs[...].reshape(PART, H))
-        hist[rows, :] = new.astype(BF)
-        store = pltpu.make_async_copy(hist.at[rows], nh_o.at[rows], out_sem.at[i])
-        store.start()
-        stores.append(store)
-
-    for i in range(4):
-        scatter(i)
+    scatter(before)
     wait_bytes(zrecv.at[pl.ds(0, Z - 1)], z_r)
     scale = BETA_MIX / (N_DOM * Y)
     asend[...] = (scale * jnp.sum(zrecv[...].astype(F32), axis=0)).astype(BF)
     for _, device in peers:
         remote(asend, arecv.at[slice_me], ag_s, ag_r, device).start()
     arecv[pl.ds(slice_me, 1)] = asend[...].reshape(1, H // GROUP, H)
-    for i in range(4, HIST // CHUNK):
-        scatter(i)
+    scatter(after)
+    for copy in on:
+        copy.wait_recv()
+    scatter(lax.rem(b + 2, Y))
 
     for copy in near_req + near_row + ring + on:
         copy.wait_send()
@@ -309,23 +294,18 @@
     wait_bytes(grecv.at[pl.ds(0, GROUP - 1)], rs_s)
     wait_bytes(zrecv.at[pl.ds(0, Z - 1)], z_s)
     wait_bytes(arecv.at[pl.ds(0, GROUP - 1)], ag_s)
-    for store in stores:
-        store.wait()
     wait_bytes(arecv.at[pl.ds(0, GROUP - 1)], ag_r)
     gw_o[...] = arecv[...].astype(F32).reshape(H, H)
 
 
-def hand_on(nh_i, gx_i, gw_i, nh_o, gx_o, gw_o, nh, gx, gw, sem_in, sem_out):
-    parts = [(nh_i.at[pl.ds(i * 1024, 1024)], nh.at[pl.ds(i * 1024, 1024)], nh_o.at[pl.ds(i * 1024, 1024)]) for i in range(4)]
-    parts = [(gw_i, gw, gw_o), (gx_i, gx, gx_o), *parts]
-    come = [pltpu.make_async_copy(src, mid, sem_in.at[i]) for i, (src, mid, _) in enumerate(parts)]
-    go = [pltpu.make_async_copy(mid, dst, sem_out.at[i]) for i, (_, mid, dst) in enumerate(parts)]
-    for copy in come:
+def hand_on(nh_i, gx_i, gw_i, nh_o, gx_o, gw_o, sem):
+    step = HIST // 4
+    parts = [(gw_i, gw_o), (gx_i, gx_o)]
+    parts += [(nh_i.at[pl.ds(i * step, step)], nh_o.at[pl.ds(i * step, step)]) for i in range(4)]
+    copies = [pltpu.make_async_copy(src, dst, sem.at[i]) for i, (src, dst) in enumerate(parts)]
+    for copy in copies:
         copy.start()
-    for first, then in zip(come, go):
-        first.wait()
-        then.start()
-    for copy in go:
+    for copy in copies:
         copy.wait()
 
 
@@ -343,33 +323,38 @@
     piece = H // GROUP
     parts = pl.pallas_call(
         kernel,
-        out_shape=shapes,
+        out_shape=(v((HIST, H), BF), v((ROWS, H), BF), v((H, H), F32)),
         in_specs=[hbm] * 9,
-        out_specs=(hbm, vmem, vmem),
+        out_specs=(vmem, vmem, vmem),
         scratch_shapes=[
             v((CAP, N_DOM), I32), v((Y, ROWS), I32), pltpu.SMEM((2, K), I32), v((HIST, H), BF), v((ROWS, H), BF),
             v((ROWS, H), BF), v((ROWS, H), BF), v((H, H), BF), v((2, K, TILE, TILE), BF),
             v((1, N_DOM), I32), v((N_DOM, 1, N_DOM), I32), v((2, CAP, N_DOM), I32),
-            v((N_DOM, 4, TILE), BF), v((N_DOM, 4, TILE), BF), v((2, CAP, H), BF), v((2, CAP, H), BF),
-            v((4 * N_DOM, 4 * N_DOM), BF), v((N_DOM * CAP, 4 * N_DOM), BF), v((N_DOM * CAP, 4 * N_DOM), BF),
-            v((N_DOM * CAP, 32), BF), v((HIST, PART), BF), v((NB, TILE, H), BF), v((ROWS, H), F32),
+            v((2, 2 * N_DOM, TILE), F32), v((N_DOM, 2, H), BF), v((N_DOM, 2, H), BF), v((2, CAP, H), BF), v((2, CAP, H), BF),
+            v((ROWS, NB * TILE), BF), v((ROWS, 2 * N_DOM), BF), v((ROWS, 32), BF), v((HIST, PART), BF),
+            v((ROWS, H), F32), v((ROWS, H), F32),
             v((Y, ROWS, H), BF), v((GROUP, piece, H), BF), v((GROUP, piece, H), BF), v((piece, H), BF),
             v((Z, piece, H), BF), v((piece, H), BF), v((GROUP, piece, H), BF),
             dma((9,)), dma(()), dma(()), dma((2,)), dma((2,)), dma(()), dma(()), dma((2,)), dma((2,)),
-            dma(()), dma(()), dma(()), dma(()), dma(()), dma(()), dma((4,)), dma((4,)), dma((HIST // CHUNK,)),
+            dma(()), dma(()), dma(()), dma(()), dma(()), dma(()), dma((4,)), dma((4,)),
         ],
-        compiler_params=pltpu.CompilerParams(collective_id=0, has_side_effects=True, vmem_limit_bytes=60 * 1024 * 1024),
+        compiler_params=pltpu.CompilerParams(collective_id=0, has_side_effects=True, vmem_limit_bytes=40 * 1024 * 1024),
         name="layer",
-    )(table, batch_ids[0], tile_cols[0, 0], history[0], features[0], initial[0], grad_output[0], weight, tile_vals[0, 0])
+    )(*[
+        pltpu.with_memory_space_constraint(a, pltpu.HBM)
+        for a in (
+            table, batch_ids[0], tile_cols[0, 0], history[0], features[0], initial[0], grad_output[0], weight, tile_vals[0, 0],
+        )
+    ])
     new_hist, grad_x, grad_w = pl.pallas_call(
         hand_on,
         out_shape=shapes,
-        in_specs=[hbm] * 3,
+        in_specs=[vmem] * 3,
         out_specs=(hbm, hbm, hbm),
-        scratch_shapes=[v((HIST, H), BF), v((ROWS, H), BF), v((H, H), F32), dma((6,)), dma((6,))],
-        compiler_params=pltpu.CompilerParams(vmem_limit_bytes=60 * 1024 * 1024),
+        scratch_shapes=[dma((6,))],
+        compiler_params=pltpu.CompilerParams(vmem_limit_bytes=16 * 1024 * 1024),
         name="hand_on",
-    )(*parts)
+    )(*[pltpu.with_memory_space_constraint(a, pltpu.VMEM) for a in parts])
     return new_hist[None], grad_x[None], grad_w
 
 

time: 61.7 us -> 58.1 us (0.942)
  Pallas kernels: 60.9 us -> 57.3 us
    pallas_call x2, Pallas kernels: 60.9 us -> 57.3 us  [the longest x1 55.8 us: shards(): pl.pallas_call(kernel, out_shape=(v((HIST, H), BF), v((ROWS, H), BF), v((...]
where the time goes in v2:
time: 58.1 us; the launch traced here: 57.9 us
  Pallas kernels  57.3 us (99%)
  between operations  0.64 us (1%)
    pallas_call x1, Pallas kernels, shards(): pl.pallas_call(kernel, out_shape=(v((HIST, H), BF), v((ROWS, H), BF), v((...  55.8 us
    pallas_call x1, Pallas kernels, shards(): pl.pallas_call(hand_on, out_shape=shapes, in_specs=[vmem] * 3, out_specs=...  1.49 us

profile of v2, /device:TPU:1, one launch (start us, length us, event | category | flops | bytes accessed | tf_op | source)
XLA Modules:
  0.0 57.9 jit_solution(11207275420879612905)
XLA Ops:
  0.6 55.8 %layer.1 = (bf16[4096,256]{1,0:T(8,128)(2,1)S(1)}, bf16[256,256]{1,0:T(8,128)(2,1)S(1)}, f32[256,256]{1,0:T(8,128)S(1)}) custom-call(s32[8,128]{1,0:T(8,128)} %bitcast.17, s32[4,256]{1,0:T(4,128)} %bitcast.18, s32[2,8]{1,0:T(2,128)} %bitcast.19, bf16[4096,256]{1,0:T(8,128)(2,1)} %bitcast.12, bf16[256,256]{1,0:T(8,128)(2,1)} %bitcast.14, ...), custom_call_target="tpu_custom_call" | custom-call | tf_op jit(solution)/shard_map/layer/pallas_call | solution.py:324
  56.4 1.5 %hand_on.1 = (bf16[4096,256]{1,0:T(8,128)(2,1)}, bf16[256,256]{1,0:T(8,128)(2,1)}, f32[256,256]{1,0:T(8,128)}) custom-call(bf16[4096,256]{1,0:T(8,128)(2,1)S(1)} %get-tuple-element.9.nh_i, bf16[256,256]{1,0:T(8,128)(2,1)S(1)} %get-tuple-element.10.gx_i, f32[256,256]{1,0:T(8,128)S(1)} %get-tuple-element.11.gw_i), custom_call_target="tpu_custom_call" | custom-call | tf_op jit(solution)/shard_map/hand_on/pallas_call | solution.py:349

commit v3 on v2

--- a/solution.py
+++ b/solution.py
@@ -122,9 +122,9 @@
     right, left = lax.rem(me + 1, N_DOM), lax.rem(me + N_DOM - 1, N_DOM)
     pl.semaphore_wait(barrier, N_DOM - 1 + len(others))
     near_req = [remote(tab, ntab.at[i], nreq_s.at[i], nreq_r.at[i], {"dom": p}) for i, p in enumerate((right, left))]
+    each_dom_peer(lambda p: remote(req, wreq.at[me], req_s, req_r, {"dom": p}).start())
     for copy in near_req:
         copy.start()
-    each_dom_peer(lambda p: remote(req, wreq.at[me], req_s, req_r, {"dom": p}).start())
 
     loads[1].wait()
 
@@ -159,22 +159,24 @@
         axis=0,
     ).astype(I32)
     n_ask = 2 * N_DOM + 32
-    got = jnp.zeros((n_ask, H), F32)
-    for i in range(HIST // CHUNK):
-        hot = ones_where(wanted == iota((n_ask, CHUNK), 1) + i * CHUNK)
-        got = got + mm(hot, hist[pl.ds(i * CHUNK, CHUNK), :])
+    block = jnp.where((wanted & 255) == iota((n_ask, 256), 1), (wanted >> 8).astype(F32), -1.0).astype(BF)
+    def part(first, last):
+        hot = jnp.concatenate([jnp.where(block[first:last] == BF(i), BF(1), BF(0)) for i in range(HIST // 256)], axis=1)
+        return mm(hot, hist[...])
+
+    got = jnp.concatenate([part(0, 144), part(144, 288)], axis=0)
     n0 = 2 * N_DOM
     nsend[0] = got[n0 + 16 : n0 + 24, :].astype(BF)
     nsend[1] = got[n0 + 8 : n0 + 16, :].astype(BF)
     near_row = [remote(nsend.at[i], nrow.at[i], nrow_s.at[i], nrow_r.at[i], {"dom": p}) for i, p in enumerate((right, left))]
-    for copy in near_row:
-        copy.start()
     for i in range(2):
         for j in range(2):
             mixed[j, pl.ds(i, N_DOM, 2), :] = got[i * N_DOM : (i + 1) * N_DOM, j * TILE : (j + 1) * TILE]
     sbuf[...] = jnp.concatenate([mixed[0], mixed[1]], axis=1).astype(BF).reshape(N_DOM, 2, H)
     rbuf[pl.ds(me, 1)] = jnp.zeros((1, 2, H), BF)
     each_dom_peer(lambda p: remote(sbuf.at[p], rbuf.at[me], row_s, row_r, {"dom": p}).start())
+    for copy in near_row:
+        copy.start()
 
     own_rows = got[n0 : n0 + 8, :]
     for i in (2, 8):

time: 58.1 us -> 57.2 us (0.985)
  Pallas kernels: 57.3 us -> 56.5 us
    pallas_call x1, Pallas kernels: 55.8 us -> 55 us  [shards(): pl.pallas_call(kernel, out_shape=(v((HIST, H), BF), v((ROWS, H), BF), v((...]
where the time goes in v3:
time: 57.2 us; the launch traced here: 57.1 us
  Pallas kernels  56.5 us (99%)
  between operations  0.64 us (1%)
    pallas_call x1, Pallas kernels, shards(): pl.pallas_call(kernel, out_shape=(v((HIST, H), BF), v((ROWS, H), BF), v((...  55 us
    pallas_call x1, Pallas kernels, shards(): pl.pallas_call(hand_on, out_shape=shapes, in_specs=[vmem] * 3, out_specs=...  1.49 us

profile of v3, /device:TPU:1, one launch (start us, length us, event | category | flops | bytes accessed | tf_op | source)
XLA Modules:
  0.0 57.1 jit_solution(7358887203067556031)
XLA Ops:
  0.6 55.0 %layer.1 = (bf16[4096,256]{1,0:T(8,128)(2,1)S(1)}, bf16[256,256]{1,0:T(8,128)(2,1)S(1)}, f32[256,256]{1,0:T(8,128)S(1)}) custom-call(s32[8,128]{1,0:T(8,128)} %bitcast.17, s32[4,256]{1,0:T(4,128)} %bitcast.18, s32[2,8]{1,0:T(2,128)} %bitcast.19, bf16[4096,256]{1,0:T(8,128)(2,1)} %bitcast.12, bf16[256,256]{1,0:T(8,128)(2,1)} %bitcast.14, ...), custom_call_target="tpu_custom_call" | custom-call | tf_op jit(solution)/shard_map/layer/pallas_call | solution.py:326
  55.6 1.5 %hand_on.1 = (bf16[4096,256]{1,0:T(8,128)(2,1)}, bf16[256,256]{1,0:T(8,128)(2,1)}, f32[256,256]{1,0:T(8,128)}) custom-call(bf16[4096,256]{1,0:T(8,128)(2,1)S(1)} %get-tuple-element.9.nh_i, bf16[256,256]{1,0:T(8,128)(2,1)S(1)} %get-tuple-element.10.gx_i, f32[256,256]{1,0:T(8,128)S(1)} %get-tuple-element.11.gw_i), custom_call_target="tpu_custom_call" | custom-call | tf_op jit(solution)/shard_map/hand_on/pallas_call | solution.py:351

commit v4 on v3

--- a/solution.py
+++ b/solution.py
@@ -22,6 +22,7 @@
 PART = Y * ROWS
 BASE = 8192
 CHUNK = 512
+FAR_PLANES = 9
 BF = jnp.bfloat16
 F32 = jnp.float32
 I32 = jnp.int32
@@ -36,22 +37,24 @@
     return (x * Z + z) * C + c
 
 
-def each_dom_peer(fn):
+def each_dom_peer(fn, first=0, last=Z):
     x, z, c, _ = coords()
 
-    def plane(zz, own):
-        for dx in (2, 1, 3, 0):
-            for dc in (1, 0):
+    def plane(zz, here, there, own):
+        for i, (dx, back) in enumerate(((2, 0), (1, 2), (3, 1), (0, 3))):
+            for j, dc in enumerate((1, 0)):
                 if not (own and dx == 0 and dc == 0):
-                    fn(dom_of(lax.rem(x + dx, X), zz, lax.rem(c + dc, C)))
+                    fn(dom_of(lax.rem(x + dx, X), zz, lax.rem(c + dc, C)), here * 8 + 2 * i + j, there * 8 + 2 * back + j)
 
     def body(k, carry):
         odd, half = lax.rem(k, 2), lax.div(k, 2)
-        plane(lax.rem(z + Z // 2 + half * (1 - 2 * odd) - odd, Z), False)
+        there = jnp.where(k == 0, 0, k + 2 * odd - 1)
+        plane(lax.rem(z + Z // 2 + half * (1 - 2 * odd) - odd, Z), k, there, False)
         return carry
 
-    lax.fori_loop(0, Z - 1, body, 0)
-    plane(z, True)
+    lax.fori_loop(first, min(last, Z - 1), body, 0)
+    if last == Z:
+        plane(z, Z - 1, Z - 1, True)
 
 
 def group_peers(skip_same_batch):
@@ -109,7 +112,7 @@
     loads = [pltpu.make_async_copy(src, dst, in_sem.at[i]) for i, (src, dst) in enumerate(pairs)]
     loads[0].start()
     barrier = pltpu.get_barrier_semaphore()
-    each_dom_peer(lambda p: pl.semaphore_signal(barrier, inc=1, device_id={"dom": p}))
+    each_dom_peer(lambda p, here, there: pl.semaphore_signal(barrier, inc=1, device_id={"dom": p}))
     others = group_peers(True)
     for _, device in others:
         pl.semaphore_signal(barrier, inc=1, device_id=device)
@@ -118,11 +121,11 @@
 
     loads[0].wait()
     req[...] = (tab[0:1, :] + 1) * BASE + (tab[1:2, :] + 1)
-    wreq[pl.ds(me, 1)] = jnp.zeros((1, 1, N_DOM), I32)
+    wreq[N_DOM - 1] = jnp.zeros((1, N_DOM), I32)
     right, left = lax.rem(me + 1, N_DOM), lax.rem(me + N_DOM - 1, N_DOM)
     pl.semaphore_wait(barrier, N_DOM - 1 + len(others))
     near_req = [remote(tab, ntab.at[i], nreq_s.at[i], nreq_r.at[i], {"dom": p}) for i, p in enumerate((right, left))]
-    each_dom_peer(lambda p: remote(req, wreq.at[me], req_s, req_r, {"dom": p}).start())
+    each_dom_peer(lambda p, here, there: remote(req, wreq.at[there], req_s, req_r, {"dom": p}).start())
     for copy in near_req:
         copy.start()
 
@@ -147,34 +150,36 @@
         return jnp.sum(jnp.where(lane_me, v.astype(F32), 0.0), axis=1, keepdims=True)
 
     asked = wreq[...].reshape(N_DOM, N_DOM)
-    wanted = jnp.concatenate(
-        [
-            column(lax.shift_right_logical(asked, 13) - 1),
-            column(jnp.bitwise_and(asked, BASE - 1) - 1),
-            column(tab[...]),
-            column(ntab[0]),
-            column(ntab[1]),
-            jnp.full((8, 1), -1.0, F32),
-        ],
-        axis=0,
-    ).astype(I32)
+    one = column(lax.shift_right_logical(asked, 13) - 1)
+    two = column(jnp.bitwise_and(asked, BASE - 1) - 1)
+    cut = FAR_PLANES * X * C
+    near_want = [column(tab[...]), column(ntab[0]), column(ntab[1]), jnp.full((8, 1), -1.0, F32)]
+    wanted = jnp.concatenate([one[:cut], two[:cut], one[cut:], two[cut:], *near_want], axis=0).astype(I32)
     n_ask = 2 * N_DOM + 32
     block = jnp.where((wanted & 255) == iota((n_ask, 256), 1), (wanted >> 8).astype(F32), -1.0).astype(BF)
     def part(first, last):
         hot = jnp.concatenate([jnp.where(block[first:last] == BF(i), BF(1), BF(0)) for i in range(HIST // 256)], axis=1)
         return mm(hot, hist[...])
 
-    got = jnp.concatenate([part(0, 144), part(144, 288)], axis=0)
-    n0 = 2 * N_DOM
+    def send_rows(rows, start, count, first, last):
+        for i in range(2):
+            for j in range(2):
+                mixed[j, pl.ds(2 * start + i, count, 2), :] = rows[i * count : (i + 1) * count, j * TILE : (j + 1) * TILE]
+        lines = slice(2 * start, 2 * (start + count))
+        both = jnp.concatenate([mixed[0, lines, :], mixed[1, lines, :]], axis=1)
+        sbuf[start : start + count] = both.astype(BF).reshape(count, 2, H)
+        each_dom_peer(
+            lambda p, here, there: remote(sbuf.at[here], rbuf.at[me], row_s, row_r, {"dom": p}).start(), first, last
+        )
+
+    rbuf[pl.ds(me, 1)] = jnp.zeros((1, 2, H), BF)
+    send_rows(part(0, 2 * cut), 0, cut, 0, FAR_PLANES)
+    got = part(2 * cut, n_ask)
+    send_rows(got, cut, N_DOM - cut, FAR_PLANES, Z)
+    n0 = 2 * (N_DOM - cut)
     nsend[0] = got[n0 + 16 : n0 + 24, :].astype(BF)
     nsend[1] = got[n0 + 8 : n0 + 16, :].astype(BF)
     near_row = [remote(nsend.at[i], nrow.at[i], nrow_s.at[i], nrow_r.at[i], {"dom": p}) for i, p in enumerate((right, left))]
-    for i in range(2):
-        for j in range(2):
-            mixed[j, pl.ds(i, N_DOM, 2), :] = got[i * N_DOM : (i + 1) * N_DOM, j * TILE : (j + 1) * TILE]
-    sbuf[...] = jnp.concatenate([mixed[0], mixed[1]], axis=1).astype(BF).reshape(N_DOM, 2, H)
-    rbuf[pl.ds(me, 1)] = jnp.zeros((1, 2, H), BF)
-    each_dom_peer(lambda p: remote(sbuf.at[p], rbuf.at[me], row_s, row_r, {"dom": p}).start())
     for copy in near_row:
         copy.start()
 

time: 57.2 us -> 57.1 us (level)
  no operation moved by 1% of the time
where the time goes in v4:
time: 57.1 us; the launch traced here: 57 us
  Pallas kernels  56.4 us (99%)
  between operations  0.64 us (1%)
    pallas_call x1, Pallas kernels, shards(): pl.pallas_call(kernel, out_shape=(v((HIST, H), BF), v((ROWS, H), BF), v((...  54.9 us
    pallas_call x1, Pallas kernels, shards(): pl.pallas_call(hand_on, out_shape=shapes, in_specs=[vmem] * 3, out_specs=...  1.49 us

profile of v4, /device:TPU:1, one launch (start us, length us, event | category | flops | bytes accessed | tf_op | source)
XLA Modules:
  0.0 57.0 jit_solution(7703339322408421389)
XLA Ops:
  0.6 54.9 %layer.1 = (bf16[4096,256]{1,0:T(8,128)(2,1)S(1)}, bf16[256,256]{1,0:T(8,128)(2,1)S(1)}, f32[256,256]{1,0:T(8,128)S(1)}) custom-call(s32[8,128]{1,0:T(8,128)} %bitcast.17, s32[4,256]{1,0:T(4,128)} %bitcast.18, s32[2,8]{1,0:T(2,128)} %bitcast.19, bf16[4096,256]{1,0:T(8,128)(2,1)} %bitcast.12, bf16[256,256]{1,0:T(8,128)(2,1)} %bitcast.14, ...), custom_call_target="tpu_custom_call" | custom-call | tf_op jit(solution)/shard_map/layer/pallas_call | solution.py:331
  55.5 1.5 %hand_on.1 = (bf16[4096,256]{1,0:T(8,128)(2,1)}, bf16[256,256]{1,0:T(8,128)(2,1)}, f32[256,256]{1,0:T(8,128)}) custom-call(bf16[4096,256]{1,0:T(8,128)(2,1)S(1)} %get-tuple-element.9.nh_i, bf16[256,256]{1,0:T(8,128)(2,1)S(1)} %get-tuple-element.10.gx_i, f32[256,256]{1,0:T(8,128)S(1)} %get-tuple-element.11.gw_i), custom_call_target="tpu_custom_call" | custom-call | tf_op jit(solution)/shard_map/hand_on/pallas_call | solution.py:356
